TPU v7x, 32 devices: a whole 2x2x4 slice. The times are simulated.
32 devices in a mesh: seg: 4 (over y, x), gx: 8 (over z, core).
Axes of the slice: x: 2, y: 2, z: 4, core: 2. Of those that a mesh axis runs over, the one named last changes fastest.
Arguments:
- start_states: float32 [4, 3, 24, 64, 384], P('seg', None, 'gx'), may hold values from -6 to 6
- base_flow: bfloat16 [4, 3, 3, 24, 64, 384], P('seg', None, None, 'gx'), may hold values from -3.5 to 3.5
Outputs:
- residual: float32 [4, 3, 24, 64, 384], P('seg', None, 'gx')
All inputs are finite; a program needn't handle non-finite values.
Results may differ from a plain program's by a relative error of at most 0.0015.
Values may be sent and summed in bfloat16 or wider, within the bound.
A program may use at most 128 MiB of HBM per device.

v0:
```python
import functools

import jax
import jax.numpy as jnp
from jax import lax
from jax.experimental import pallas as pl
from jax.experimental.pallas import tpu as pltpu
from jax.sharding import PartitionSpec as P

TIME_STEP = 0.3
VISCOSITY = 0.45
MESH = pl.DeviceIdType.MESH
ROWS = 16
EXCHANGED = (0,)
PAD_Q = 8
PAD_B = 16
F32 = jnp.float32
BF16 = jnp.bfloat16


def encode(values):
    square = values * values
    fourth = square * square
    eighth = fourth * fourth
    return jnp.where(values < 0, -eighth, eighth).astype(BF16)


def decode(code):
    code = code.astype(F32)
    size = jnp.sqrt(jnp.sqrt(jnp.sqrt(jnp.abs(code))))
    return jnp.where(code < 0, -size, size)


def kernel(n_seg, n_gx, steps, nl, ny, nz, start_ref, base_ref, out_ref, q, b, hq, hb, sq, enc, ra, rb, tq, tgt,
           load_sem, qs_sem, qr_sem, fs_sem, fr_sem, bs_sem, br_sem, shift_sem, a_sem, ar_sem, b_sem, c_sem, cr_sem):
    seg = lax.axis_index("seg")
    gx = lax.axis_index("gx")
    last = n_seg - 1
    left, right = lax.rem(gx + n_gx - 1, n_gx), lax.rem(gx + 1, n_gx)
    across = lax.rem(gx + n_gx // 2, n_gx)
    relays = (0, 1, 2, last)
    quarter = ny // 4

    load_q = pltpu.make_async_copy(start_ref.at[0], q.at[0, :, :, pl.ds(PAD_Q, ny), :], load_sem.at[0])
    load_q.start()
    load_b = [
        pltpu.make_async_copy(base_ref.at[0, k], b.at[k, :, :, pl.ds(PAD_B, ny), :], load_sem.at[1 + k])
        for k in range(steps)
    ]
    for copy in load_b:
        copy.start()

    barrier = pltpu.get_barrier_semaphore()
    for other in (left, right, across):
        pl.semaphore_signal(barrier, inc=1, device_id={"gx": other}, device_id_type=MESH)
    for d in range(1, n_seg):
        pl.semaphore_signal(barrier, inc=1, device_id={"seg": lax.rem(seg + d, n_seg)}, device_id_type=MESH)

    def comps(k):
        return pl.ds(0, 1 if k in EXCHANGED else 3)

    def q_copy(k, side):
        return pltpu.make_async_remote_copy(
            src_ref=sq.at[k, side, comps(k)], dst_ref=hq.at[k, side, comps(k)],
            send_sem=qs_sem.at[k, side], recv_sem=qr_sem.at[k, side],
            device_id={"gx": right if side == 0 else left}, device_id_type=MESH)

    def f_copy(k, side):
        return pltpu.make_async_remote_copy(
            src_ref=sq.at[k, side, pl.ds(1, 2)], dst_ref=hq.at[k, side, pl.ds(1, 2)],
            send_sem=fs_sem.at[k, side], recv_sem=fr_sem.at[k, side],
            device_id={"gx": right if side == 0 else left}, device_id_type=MESH)

    def b_copy(k, side):
        return pltpu.make_async_remote_copy(
            src_ref=base_ref.at[0, k, comps(k), nl - 1 if side == 0 else 0], dst_ref=hb.at[k, side, comps(k)],
            send_sem=bs_sem.at[k, side], recv_sem=br_sem.at[k, side],
            device_id={"gx": right if side == 0 else left}, device_id_type=MESH)

    shift = pltpu.make_async_remote_copy(
        src_ref=start_ref.at[0], dst_ref=tgt, send_sem=shift_sem.at[0], recv_sem=shift_sem.at[1],
        device_id={"seg": lax.rem(seg + n_seg - 1, n_seg)}, device_id_type=MESH)

    def a_copy(j):
        return pltpu.make_async_remote_copy(
            src_ref=enc.at[j], dst_ref=ra, send_sem=a_sem.at[j], recv_sem=ar_sem.at[0],
            device_id={"seg": relays[j]}, device_id_type=MESH)

    def z_copy(source):
        return pltpu.make_async_remote_copy(
            src_ref=source, dst_ref=rb, send_sem=b_sem.at[0], recv_sem=b_sem.at[1],
            device_id={"gx": across}, device_id_type=MESH)

    def c_copy(j):
        return pltpu.make_async_remote_copy(
            src_ref=rb, dst_ref=tq.at[j], send_sem=c_sem.at[0], recv_sem=cr_sem.at[j],
            device_id={"seg": last}, device_id_type=MESH)

    q[:, :, :, 0:PAD_Q, :] = jnp.zeros((2, 3, nl, PAD_Q, nz), F32)
    q[:, :, :, PAD_Q + ny:, :] = jnp.zeros((2, 3, nl, PAD_Q, nz), F32)
    for c in range(3):
        wall = jnp.full((steps, nl, PAD_B, nz), 1.0 if c == 0 else 0.0, BF16)
        b[:, c, :, 0:PAD_B, :] = -wall
        b[:, c, :, PAD_B + ny:, :] = wall

    load_q.wait()
    for c in range(1 if 0 in EXCHANGED else 3):
        sq[0, 0, c] = q[0, c, nl - 1, PAD_Q:PAD_Q + ny, :].astype(BF16)
        sq[0, 1, c] = q[0, c, 0, PAD_Q:PAD_Q + ny, :].astype(BF16)
    pl.semaphore_wait(barrier, 3 + n_seg - 1)
    for side in range(2):
        b_copy(0, side).start()
        q_copy(0, side).start()

    @pl.when(seg == 0)
    def _():
        for j in range(4):
            for c in range(3):
                enc[j, c] = encode(q[0, c, :, PAD_Q + j * quarter:PAD_Q + (j + 1) * quarter, :])
        for j in range(1, 4):
            a_copy(j).start()

    @pl.when(seg > 0)
    def _():
        shift.start()

    def q_window(slot, c, x, at):
        window = q[slot, c, x, pl.ds(at, ROWS + 2 * PAD_Q), :]
        return window[PAD_Q:PAD_Q + ROWS], window

    def shifted(window, pad):
        size = window.shape[0]
        up = pltpu.roll(window, size - 1, 0)[pad:pad + ROWS]
        down = pltpu.roll(window, 1, 0)[pad:pad + ROWS]
        return up, down

    half = 0.5 * TIME_STEP
    diffuse = TIME_STEP * VISCOSITY

    def layer(k, x):
        slot = k % 2

        def chunk(r, carry):
            at = pl.multiple_of(r * ROWS, ROWS)
            here = pl.ds(at, ROWS)

            def q_side(c, side):
                neighbour = x + (-1 if side == 0 else 1)
                return q[slot, c, neighbour, pl.ds(at + PAD_Q, ROWS), :]

            def b_side(c, side):
                neighbour = x + (-1 if side == 0 else 1)
                return b[k, c, neighbour, pl.ds(at + PAD_B, ROWS), :].astype(F32)

            windows = [b[k, c, x, pl.ds(at, ROWS + 2 * PAD_B), :].astype(F32) for c in range(3)]
            carried = [half * window[PAD_B:PAD_B + ROWS] for window in windows]
            ahead = [diffuse - value for value in carried]
            behind = [diffuse + value for value in carried]
            centres = [q[slot, c, x, pl.ds(at + PAD_Q, ROWS), :] for c in range(3)]
            pushed = [half * value for value in centres]
            for c in range(3):
                centre, window = q_window(slot, c, x, at)
                up, down = shifted(window, PAD_Q)
                total = (1.0 - 6.0 * diffuse) * centre
                if x < nl - 1:
                    total += ahead[0] * q_side(c, 1) - pushed[0] * b_side(c, 1)
                if x > 0:
                    total += behind[0] * q_side(c, 0) + pushed[0] * b_side(c, 0)
                total += ahead[1] * up + behind[1] * down
                total += ahead[2] * pltpu.roll(centre, nz - 1, 1) + behind[2] * pltpu.roll(centre, 1, 1)
                base = windows[c][PAD_B - 8:PAD_B + ROWS + 8]
                up, down = shifted(base, 8)
                total -= pushed[1] * (up - down)
                base = windows[c][PAD_B:PAD_B + ROWS]
                total -= pushed[2] * (pltpu.roll(base, nz - 1, 1) - pltpu.roll(base, 1, 1))
                if k == steps - 1:
                    out_ref[0, c, x, here, :] = total
                else:
                    q[1 - slot, c, x, pl.ds(at + PAD_Q, ROWS), :] = total
            return carry

        lax.fori_loop(0, ny // ROWS, chunk, 0, unroll=True)

    def close(k, side):
        slot = k % 2
        x = 0 if side == 0 else nl - 1

        def chunk(r, carry):
            at = pl.multiple_of(r * ROWS, ROWS)
            here = pl.ds(at, ROWS)
            inner = pl.ds(at + PAD_Q, ROWS)
            carried = half * b[k, 0, x, pl.ds(at + PAD_B, ROWS), :].astype(F32)
            pushed = half * q[slot, 0, x, inner, :]
            weight = diffuse + carried if side == 0 else diffuse - carried
            for c in range(3):
                gained = hq[k, side, c, here, :].astype(F32)
                if c == 0 or k not in EXCHANGED:
                    pressed = pushed * hb[k, side, c, here, :].astype(F32)
                    gained = weight * gained + pressed if side == 0 else weight * gained - pressed
                if k == steps - 1:
                    out_ref[0, c, x, here, :] += gained - tgt[c, x, here, :]
                else:
                    total = q[1 - slot, c, x, inner, :] + gained
                    q[1 - slot, c, x, inner, :] = total
                    if c == 0 or k + 1 not in EXCHANGED:
                        sq[k + 1, 1 - side, c, here, :] = total.astype(BF16)
            return carry

        lax.fori_loop(0, ny // ROWS, chunk, 0, unroll=True)

    def contribute(k, side):
        slot = k % 2
        x = 0 if side == 0 else nl - 1

        def chunk(r, carry):
            at = pl.multiple_of(r * ROWS, ROWS)
            here = pl.ds(at, ROWS)
            carried = half * hb[k, side, 0, here, :].astype(F32)
            pushed = half * hq[k, side, 0, here, :].astype(F32)
            for c in range(1, 3):
                mine = q[slot, c, x, pl.ds(at + PAD_Q, ROWS), :]
                base = b[k, c, x, pl.ds(at + PAD_B, ROWS), :].astype(F32)
                if side == 0:
                    share = (diffuse - carried) * mine - pushed * base
                else:
                    share = (diffuse + carried) * mine + pushed * base
                sq[k, 1 - side, c, here, :] = share.astype(BF16)
            return carry

        lax.fori_loop(0, ny // ROWS, chunk, 0, unroll=True)

    def is_relay():
        flag = seg == 0
        for r in relays[1:]:
            flag = flag | (seg == r)
        return flag

    def finish_target():
        @pl.when(seg < last)
        def _():
            shift.wait_recv()

        @pl.when(seg == last)
        def _():
            z_copy(ra).wait_recv()
            for j in range(3):
                c_copy(j).wait_recv()
            row = lax.broadcasted_iota(jnp.int32, (nz, nz), 0)
            column = lax.broadcasted_iota(jnp.int32, (nz, nz), 1)
            flip = jnp.where((row + column == 0) | (row + column == nz), 1.0, 0.0).astype(BF16)
            for j in range(4):
                source = rb if j == 3 else tq.at[j]
                for c in range(3):
                    values = decode(source[c]).reshape(nl * quarter, nz)
                    high = values.astype(BF16)
                    low = (values - high.astype(F32)).astype(BF16)
                    flipped = jnp.dot(high, flip, preferred_element_type=F32)
                    flipped += jnp.dot(low, flip, preferred_element_type=F32)
                    if c == 2:
                        flipped = -flipped
                    tgt[c, :, j * quarter:(j + 1) * quarter, :] = flipped.reshape(nl, quarter, nz)

    def start_relay():
        @pl.when(seg == 0)
        def _():
            z_copy(enc.at[0]).start()

        @pl.when((seg != 0) & is_relay())
        def _():
            a_copy(0).wait_recv()
            z_copy(ra).start()

    def sent(k):
        for side in range(2):
            q_copy(k, side).wait_send()
            b_copy(k, side).wait_send()
        if k + 1 < steps:
            for side in range(2):
                b_copy(k + 1, side).start()

    def arrived(k, side):
        q_copy(k, side).wait_recv()
        b_copy(k, side).wait_recv()

    for k in range(steps):
        load_b[k].wait()
        exchanged = k in EXCHANGED
        for x in range(nl):
            layer(k, x)
            if x == (0 if exchanged else nl - 2):
                sent(k)
        if exchanged:
            for side in range(2):
                arrived(k, side)
                contribute(k, side)
                f_copy(k, 1 - side).start()
        if k == 0:
            start_relay()
        if exchanged:
            for side in range(2):
                f_copy(k, side).wait_send()

        if k == steps - 1:
            finish_target()
            for x in range(1, nl - 1):
                for c in range(3):
                    out_ref[0, c, x] -= tgt[c, x]
        for side in range(2):
            if exchanged:
                f_copy(k, side).wait_recv()
            else:
                arrived(k, side)
            close(k, side)
            if k < steps - 1:
                q_copy(k + 1, 1 - side).start()
        if k == steps - 2:
            @pl.when(is_relay() & (seg != last))
            def _():
                z_copy(ra).wait_recv()
                for j in range(3):
                    @pl.when(seg == relays[j])
                    def _():
                        c_copy(j).start()

    @pl.when(seg > 0)
    def _():
        shift.wait_send()

    @pl.when(seg == 0)
    def _():
        for j in range(1, 4):
            a_copy(j).wait_send()

    @pl.when(is_relay())
    def _():
        z_copy(ra).wait_send()

    @pl.when(is_relay() & (seg != last))
    def _():
        c_copy(0).wait_send()


def local(n_seg, n_gx, start_states, base_flow):
    _, _, nl, ny, nz = start_states.shape
    steps = base_flow.shape[1]
    quarter = ny // 4
    dma = pltpu.SemaphoreType.DMA
    return pl.pallas_call(
        functools.partial(kernel, n_seg, n_gx, steps, nl, ny, nz),
        out_shape=jax.ShapeDtypeStruct(start_states.shape, F32),
        in_specs=[pl.BlockSpec(memory_space=pltpu.HBM)] * 2,
        out_specs=pl.BlockSpec(memory_space=pltpu.VMEM),
        scratch_shapes=[
            pltpu.VMEM((2, 3, nl, ny + 2 * PAD_Q, nz), F32),
            pltpu.VMEM((steps, 3, nl, ny + 2 * PAD_B, nz), BF16),
            pltpu.VMEM((steps, 2, 3, ny, nz), BF16),
            pltpu.VMEM((steps, 2, 3, ny, nz), BF16),
            pltpu.VMEM((steps, 2, 3, ny, nz), BF16),
            pltpu.VMEM((4, 3, nl, quarter, nz), BF16),
            pltpu.VMEM((3, nl, quarter, nz), BF16),
            pltpu.VMEM((3, nl, quarter, nz), BF16),
            pltpu.VMEM((3, 3, nl, quarter, nz), BF16),
            pltpu.VMEM((3, nl, ny, nz), F32),
            dma((1 + steps,)),
            dma((steps, 2)), dma((steps, 2)),
            dma((steps, 2)), dma((steps, 2)),
            dma((steps, 2)), dma((steps, 2)),
            dma((2,)),
            dma((4,)), dma((1,)),
            dma((2,)),
            dma((1,)), dma((3,)),
        ],
        compiler_params=pltpu.CompilerParams(
            collective_id=0, has_side_effects=True, vmem_limit_bytes=44 * 1024 * 1024),
        cost_estimate=pl.CostEstimate(flops=60_000_000, bytes_accessed=4_000_000, transcendentals=0),
    )(pltpu.with_memory_space_constraint(start_states, pltpu.HBM), pltpu.with_memory_space_constraint(base_flow, pltpu.HBM))


def solution(mesh):
    in_specs = (P("seg", None, "gx", None, None), P("seg", None, None, "gx", None, None))
    out_specs = P("seg", None, "gx", None, None)
    body = functools.partial(local, mesh.shape["seg"], mesh.shape["gx"])
    return jax.shard_map(body, mesh=mesh, in_specs=in_specs, out_specs=out_specs, check_vma=False)
```

profile of v0, /device:TPU:9, one launch (start us, length us, event | category | flops | bytes accessed | tf_op | source)
XLA Modules:
  0.0 30.2 jit_solution(17785994850171618936)
XLA Ops:
  0.0 29.2 %shard_map.28 = f32[1,3,3,64,384]{4,3,2,1,0:T(8,128)S(1)} custom-call(f32[1,3,3,64,384]{4,3,2,1,0:T(8,128)} %start_ref.1, bf16[1,3,3,3,64,384]{5,4,3,2,1,0:T(8,128)(2,1)} %base_ref.1), custom_call_target="tpu_custom_call" | custom-call | flops 60000000 | bytes 4000000 | tf_op jit(solution)/shard_map/pallas_call | solution.py:348
  29.3 0.9 %copy.4 = f32[1,3,3,64,384]{4,3,2,1,0:T(8,128)} copy(f32[1,3,3,64,384]{4,3,2,1,0:T(8,128)S(1)} %shard_map.28) | data formatting | bytes 1769472
where the time goes:
time: 30.3 us; the launch traced here: 30.2 us
  Pallas kernels  29.2 us (96%)
  local copies, waits for them, and re-layouts  0.91 us (3%)
    pallas_call x1, Pallas kernels, local(): pl.pallas_call(functools.partial(kernel, n_seg, n_gx, steps, nl, ny, nz),...  29.2 us
    unnamed x1, local copies, waits for them, and re-layouts  0.91 us

commit v1 on v0

v1 whole, which is shorter than its diff:
```python
import functools

import jax
import jax.numpy as jnp
from jax import lax
from jax.experimental import pallas as pl
from jax.experimental.pallas import tpu as pltpu
from jax.sharding import PartitionSpec as P

TIME_STEP = 0.3
VISCOSITY = 0.45
HALF = 0.5 * TIME_STEP
DIFFUSE = TIME_STEP * VISCOSITY
MESH = pl.DeviceIdType.MESH
ROWS = 16
PAD_Q = 8
PAD_B = 16
RELAY_AT = 1
F32 = jnp.float32
BF16 = jnp.bfloat16

PLANES = {"Q0": (0, 1), "S0": (1, 1), "G": (2, 2), "U": (4, 1), "H": (5, 2), "L": (7, 2)}
KINDS = tuple(PLANES)


def encode(values):
    square = values * values
    fourth = square * square
    eighth = fourth * fourth
    return jnp.where(values < 0, -eighth, eighth).astype(BF16)


def decode(code):
    code = code.astype(F32)
    size = jnp.sqrt(jnp.sqrt(jnp.sqrt(jnp.abs(code))))
    return jnp.where(code < 0, -size, size)


def kernel(n_seg, n_gx, nl, ny, nz, start_ref, base_ref, out_ref, q, b, hq, hb, sq, nq, ub, gp, enc, rt, ra, rb, tq,
           load_sem, qs_sem, qr_sem, bs_sem, br_sem, shift_sem, a_sem, ar_sem, b_sem, c_sem, cr_sem):
    seg = lax.axis_index("seg")
    gx = lax.axis_index("gx")
    last = n_seg - 1
    left, right = lax.rem(gx + n_gx - 1, n_gx), lax.rem(gx + 1, n_gx)
    across = lax.rem(gx + n_gx // 2, n_gx)
    relays = (0, 1, 2, last)
    quarter = ny // 4
    far = lax.rem(gx, 2)
    near = 1 - far
    inner_rows = pl.ds(PAD_B, ny)

    def edge(s):
        return s * (nl - 1)

    load_q = pltpu.make_async_copy(start_ref.at[0], q.at[0, :, :, pl.ds(PAD_Q, ny), :], load_sem.at[0])
    load_q.start()
    load_b = [
        pltpu.make_async_copy(base_ref.at[0, k], b.at[k, :, :, inner_rows, :], load_sem.at[1 + k]) for k in range(3)
    ]
    for copy in load_b:
        copy.start()

    barrier = pltpu.get_barrier_semaphore()
    for other in (left, right, across):
        pl.semaphore_signal(barrier, inc=1, device_id={"gx": other}, device_id_type=MESH)
    for d in range(1, n_seg):
        pl.semaphore_signal(barrier, inc=1, device_id={"seg": lax.rem(seg + d, n_seg)}, device_id_type=MESH)

    def neighbour(s):
        return {"gx": lax.rem(gx + n_gx - 1 + 2 * s, n_gx)}

    def q_copy(kind, s):
        first, count = PLANES[kind]
        at, i = pl.ds(first, count), KINDS.index(kind)
        return pltpu.make_async_remote_copy(
            src_ref=sq.at[s, at], dst_ref=hq.at[1 - s, at], send_sem=qs_sem.at[i, s], recv_sem=qr_sem.at[i, 1 - s],
            device_id=neighbour(s), device_id_type=MESH)

    def b_copy(k, s):
        return pltpu.make_async_remote_copy(
            src_ref=base_ref.at[0, k, 0, edge(s)], dst_ref=hb.at[1 - s, k, inner_rows],
            send_sem=bs_sem.at[k, s], recv_sem=br_sem.at[k, 1 - s],
            device_id=neighbour(s), device_id_type=MESH)

    shift = pltpu.make_async_remote_copy(
        src_ref=enc, dst_ref=rt, send_sem=shift_sem.at[0], recv_sem=shift_sem.at[1],
        device_id={"seg": lax.rem(seg + n_seg - 1, n_seg)}, device_id_type=MESH)

    def a_copy(j):
        return pltpu.make_async_remote_copy(
            src_ref=enc.at[j], dst_ref=ra, send_sem=a_sem.at[j], recv_sem=ar_sem.at[0],
            device_id={"seg": relays[j]}, device_id_type=MESH)

    def z_copy(source):
        return pltpu.make_async_remote_copy(
            src_ref=source, dst_ref=rb, send_sem=b_sem.at[0], recv_sem=b_sem.at[1],
            device_id={"gx": across}, device_id_type=MESH)

    def c_copy(j):
        return pltpu.make_async_remote_copy(
            src_ref=rb, dst_ref=tq.at[j], send_sem=c_sem.at[0], recv_sem=cr_sem.at[j],
            device_id={"seg": last}, device_id_type=MESH)

    q[:, :, :, 0:PAD_Q, :] = jnp.zeros((2, 3, nl, PAD_Q, nz), F32)
    q[:, :, :, PAD_Q + ny:, :] = jnp.zeros((2, 3, nl, PAD_Q, nz), F32)
    for c in range(3):
        wall = jnp.full((3, nl, PAD_B, nz), 1.0 if c == 0 else 0.0, BF16)
        b[:, c, :, 0:PAD_B, :] = -wall
        b[:, c, :, PAD_B + ny:, :] = wall
    wall = jnp.full((2, PAD_B, nz), 1.0, BF16)
    hb[:, 1, 0:PAD_B, :] = -wall
    hb[:, 1, PAD_B + ny:, :] = wall

    load_q.wait()
    for s in range(2):
        sq[s, 0] = q[0, 0, edge(s), PAD_Q:PAD_Q + ny, :].astype(BF16)
    pl.semaphore_wait(barrier, 3 + n_seg - 1)
    for s in (far, near):
        b_copy(0, s).start()
        q_copy("Q0", s).start()

    def by_rows(chunk):
        def body(r, carry):
            chunk(pl.multiple_of(r * ROWS, ROWS))
            return carry

        lax.fori_loop(0, ny // ROWS, body, 0, unroll=True)

    def sign(s):
        return jnp.where(s == 0, HALF, -HALF).astype(F32)

    def shifted(window, pad):
        size = window.shape[0]
        up = pltpu.roll(window, size - 1, 0)[pad:pad + ROWS]
        down = pltpu.roll(window, 1, 0)[pad:pad + ROWS]
        return up, down

    def slopes(window):
        up, down = shifted(window[PAD_B - 8:PAD_B + ROWS + 8], 8)
        base = window[PAD_B:PAD_B + ROWS]
        return up - down, pltpu.roll(base, nz - 1, 1) - pltpu.roll(base, 1, 1)

    def q_at(k, c, x, at):
        return q[k % 2, c, x, pl.ds(at + PAD_Q, ROWS), :]

    def b_at(k, c, x, at):
        return b[k, c, x, pl.ds(at + PAD_B, ROWS), :].astype(F32)

    def hb_at(s, k, at):
        return hb[s, k, pl.ds(at + PAD_B, ROWS), :].astype(F32)

    def hq_at(s, i, at):
        return hq[s, i, pl.ds(at, ROWS), :].astype(F32)

    def stencil(k, x, at, comps, side=None):
        slot = k % 2
        windows = [b[k, c, x, pl.ds(at, ROWS + 2 * PAD_B), :].astype(F32) for c in range(3)]
        carried = [HALF * window[PAD_B:PAD_B + ROWS] for window in windows]
        ahead = [DIFFUSE - value for value in carried]
        behind = [DIFFUSE + value for value in carried]
        centres = [q_at(k, c, x, at) for c in range(3)]
        pushed = [HALF * value for value in centres]
        if side is not None:
            towards = 2.0 * sign(side) / TIME_STEP
            weight = DIFFUSE - towards * carried[0]
            push = towards * pushed[0]
            inward = x + 1 - 2 * side
        totals = []
        for c in comps:
            window = q[slot, c, x, pl.ds(at, ROWS + 2 * PAD_Q), :]
            centre = centres[c]
            up, down = shifted(window, PAD_Q)
            total = (1.0 - 6.0 * DIFFUSE) * centre
            if side is None:
                total += ahead[0] * q_at(k, c, x + 1, at) - pushed[0] * b_at(k, c, x + 1, at)
                total += behind[0] * q_at(k, c, x - 1, at) + pushed[0] * b_at(k, c, x - 1, at)
            else:
                total += weight * q_at(k, c, inward, at) - push * b_at(k, c, inward, at)
            total += ahead[1] * up + behind[1] * down
            total += ahead[2] * pltpu.roll(centre, nz - 1, 1) + behind[2] * pltpu.roll(centre, 1, 1)
            rise, run = slopes(windows[c])
            total -= pushed[1] * rise
            total -= pushed[2] * run
            totals.append(total)
        return totals

    def inner(k, x):
        def chunk(at):
            for c, total in enumerate(stencil(k, x, at, range(3))):
                if k == 2:
                    out_ref[0, c, x, pl.ds(at, ROWS), :] = total
                else:
                    q[1 - k % 2, c, x, pl.ds(at + PAD_Q, ROWS), :] = total

        by_rows(chunk)

    def first(s):
        x = edge(s)

        def chunk(at):
            totals = stencil(0, x, at, range(3), s)
            for c in range(3):
                q[1, c, x, pl.ds(at + PAD_Q, ROWS), :] = totals[c]
            sq[s, 1, pl.ds(at, ROWS), :] = totals[0].astype(BF16)

        by_rows(chunk)
        q_copy("S0", s).start()
        b_copy(1, s).start()

    def exchange(s):
        x, signed = edge(s), sign(s)
        b_copy(0, 1 - s).wait_recv()
        q_copy("Q0", 1 - s).wait_recv()

        def chunk(at):
            here, inside = pl.ds(at, ROWS), pl.ds(at + PAD_Q, ROWS)
            carried, pushed = signed * hb_at(s, 0, at), hq_at(s, 0, at)
            weight, push = DIFFUSE - carried, signed * pushed
            mine, base = q_at(0, 0, x, at), b_at(0, 0, x, at)
            nq[s, here, :] = weight * mine - push * base
            q[1, 0, x, inside, :] += (DIFFUSE + signed * base) * pushed + mine * carried
            for c in range(1, 3):
                share = weight * q_at(0, c, x, at) - push * b_at(0, c, x, at)
                sq[s, 1 + c, here, :] = share.astype(BF16)

        by_rows(chunk)
        q_copy("G", s).start()

    def ahead_of(s):
        x = edge(s)

        def chunk(at):
            total, = stencil(1, x, at, range(1), s)
            ub[s, pl.ds(at, ROWS), :] = total
            sq[s, 4, pl.ds(at, ROWS), :] = total.astype(BF16)

        by_rows(chunk)
        q_copy("U", s).start()

    def second(s):
        x, signed = edge(s), sign(s)
        b_copy(1, 1 - s).wait_recv()
        q_copy("S0", 1 - s).wait_recv()

        def chunk(at):
            here = pl.ds(at, ROWS)
            theirs = nq[s, here, :] + hq_at(s, 1, at)
            nq[s, here, :] = theirs
            weight, push = DIFFUSE - signed * hb_at(s, 1, at), signed * theirs
            for c in range(1, 3):
                share = weight * q_at(1, c, x, at) - push * b_at(1, c, x, at)
                sq[s, 4 + c, here, :] = share.astype(BF16)

        by_rows(chunk)
        q_copy("H", s).start()

    def prepare(s):
        x, signed = edge(s), sign(s)

        def chunk(at):
            here = pl.ds(at, ROWS)
            theirs = nq[s, here, :]
            window = hb[s, 1, pl.ds(at, ROWS + 2 * PAD_B), :].astype(F32)
            carried = signed * window[PAD_B:PAD_B + ROWS]
            mine, base = q_at(1, 0, x, at), b_at(1, 0, x, at)
            weight = DIFFUSE + signed * base
            ub[s, here, :] += weight * theirs + mine * carried
            shares = [sq[s, 1 + c, here, :].astype(F32) for c in range(1, 3)]
            rise, run = slopes(window)
            kept = (DIFFUSE - carried) * mine - (signed * theirs) * base
            nq[s, here, :] = kept - HALF * (shares[0] * rise + shares[1] * run)
            for c in range(2):
                gp[s, c, here, :] = weight * shares[c]

        by_rows(chunk)

    def third(s):
        x, signed = edge(s), sign(s)
        q_copy("G", 1 - s).wait_recv()

        def add(at):
            here, inside = pl.ds(at, ROWS), pl.ds(at + PAD_Q, ROWS)
            shares = [hq_at(s, 1 + c, at) for c in range(1, 3)]
            rise, run = slopes(b[1, 0, x, pl.ds(at, ROWS + 2 * PAD_B), :].astype(F32))
            q[0, 0, x, inside, :] = ub[s, here, :] - HALF * (shares[0] * rise + shares[1] * run)
            for c in range(1, 3):
                q[1, c, x, inside, :] += shares[c - 1]

        by_rows(add)
        q_copy("U", 1 - s).wait_recv()
        q_copy("H", 1 - s).wait_recv()
        b_copy(2, 1 - s).wait_recv()

        def chunk(at):
            here, inside = pl.ds(at, ROWS), pl.ds(at + PAD_Q, ROWS)
            theirs = nq[s, here, :] + hq_at(s, 4, at)
            nq[s, here, :] = theirs
            weight, push = DIFFUSE - signed * hb_at(s, 2, at), signed * theirs
            for c, total in zip((1, 2), stencil(1, x, at, (1, 2), s)):
                total += gp[s, c - 1, here, :] + hq_at(s, 4 + c, at)
                q[0, c, x, inside, :] = total
                sq[s, 6 + c, here, :] = (weight * total - push * b_at(2, c, x, at)).astype(BF16)

        by_rows(chunk)
        q_copy("L", s).start()

    def final(s):
        x, signed = edge(s), sign(s)

        def chunk(at):
            here = pl.ds(at, ROWS)
            totals = stencil(2, x, at, range(3), s)
            carried = signed * b_at(2, 0, x, at)
            totals[0] += (DIFFUSE + carried) * nq[s, here, :] + (signed * q_at(2, 0, x, at)) * hb_at(s, 2, at)
            for c in range(3):
                out_ref[0, c, x, here, :] = totals[c]

        by_rows(chunk)

    def close(s):
        x = edge(s)
        q_copy("L", 1 - s).wait_recv()

        def chunk(at):
            for c in range(1, 3):
                out_ref[0, c, x, pl.ds(at, ROWS), :] += hq_at(s, 6 + c, at)

        by_rows(chunk)

    def is_relay():
        flag = seg == 0
        for r in relays[1:]:
            flag = flag | (seg == r)
        return flag

    def start_relay():
        @pl.when(seg == 0)
        def _():
            z_copy(enc.at[0]).start()

        @pl.when((seg != 0) & is_relay())
        def _():
            a_copy(0).wait_recv()
            z_copy(ra).start()

    def forward_relay():
        @pl.when(is_relay() & (seg != last))
        def _():
            z_copy(ra).wait_recv()
            for j in range(3):
                @pl.when(seg == relays[j])
                def _():
                    c_copy(j).start()

    def subtract_target():
        @pl.when(seg < last)
        def _():
            shift.wait_recv()
            for j in range(4):
                for c in range(3):
                    out_ref[0, c, :, j * quarter:(j + 1) * quarter, :] -= decode(rt[j, c])

        @pl.when(seg == last)
        def _():
            z_copy(ra).wait_recv()
            for j in range(3):
                c_copy(j).wait_recv()
            row = lax.broadcasted_iota(jnp.int32, (nz, nz), 0)
            column = lax.broadcasted_iota(jnp.int32, (nz, nz), 1)
            flip = jnp.where((row + column == 0) | (row + column == nz), 1.0, 0.0).astype(BF16)
            for j in range(4):
                source = rb if j == 3 else tq.at[j]
                for c in range(3):
                    values = decode(source[c]).reshape(nl * quarter, nz)
                    high = values.astype(BF16)
                    low = (values - high.astype(F32)).astype(BF16)
                    flipped = jnp.dot(high, flip, preferred_element_type=F32)
                    flipped += jnp.dot(low, flip, preferred_element_type=F32)
                    if c == 2:
                        flipped = -flipped
                    out_ref[0, c, :, j * quarter:(j + 1) * quarter, :] -= flipped.reshape(nl, quarter, nz)

    for j in range(4):
        for c in range(3):
            enc[j, c] = encode(q[0, c, :, PAD_Q + j * quarter:PAD_Q + (j + 1) * quarter, :])

    @pl.when(seg == 0)
    def _():
        for j in range(1, 4):
            a_copy(j).start()

    @pl.when(seg > 0)
    def _():
        shift.start()

    load_b[0].wait()
    first(far)
    first(near)
    for x in range(1, nl - 1):
        inner(0, x)
    load_b[1].wait()
    exchange(near)
    exchange(far)
    if RELAY_AT == 0:
        start_relay()
    ahead_of(far)
    ahead_of(near)
    if RELAY_AT == 1:
        start_relay()
    second(near)
    second(far)
    b_copy(2, far).start()
    b_copy(2, near).start()
    if RELAY_AT == 2:
        start_relay()
    prepare(near)
    prepare(far)
    load_b[2].wait()
    third(near)
    third(far)
    for x in range(1, nl - 1):
        inner(1, x)
    forward_relay()
    final(near)
    final(far)
    for x in range(1, nl - 1):
        inner(2, x)
    subtract_target()
    close(near)
    close(far)

    for s in range(2):
        for kind in KINDS:
            q_copy(kind, s).wait_send()
        for k in range(3):
            b_copy(k, s).wait_send()

    @pl.when(seg > 0)
    def _():
        shift.wait_send()

    @pl.when(seg == 0)
    def _():
        for j in range(1, 4):
            a_copy(j).wait_send()

    @pl.when(is_relay())
    def _():
        z_copy(ra).wait_send()

    @pl.when(is_relay() & (seg != last))
    def _():
        c_copy(0).wait_send()


def local(n_seg, n_gx, start_states, base_flow):
    _, _, nl, ny, nz = start_states.shape
    assert base_flow.shape[1] == 3 and nl >= 3
    quarter = ny // 4
    dma = pltpu.SemaphoreType.DMA
    return pl.pallas_call(
        functools.partial(kernel, n_seg, n_gx, nl, ny, nz),
        out_shape=jax.ShapeDtypeStruct(start_states.shape, F32),
        in_specs=[pl.BlockSpec(memory_space=pltpu.HBM)] * 2,
        out_specs=pl.BlockSpec(memory_space=pltpu.VMEM),
        scratch_shapes=[
            pltpu.VMEM((2, 3, nl, ny + 2 * PAD_Q, nz), F32),
            pltpu.VMEM((3, 3, nl, ny + 2 * PAD_B, nz), BF16),
            pltpu.VMEM((2, 9, ny, nz), BF16),
            pltpu.VMEM((2, 3, ny + 2 * PAD_B, nz), BF16),
            pltpu.VMEM((2, 9, ny, nz), BF16),
            pltpu.VMEM((2, ny, nz), F32),
            pltpu.VMEM((2, ny, nz), F32),
            pltpu.VMEM((2, 2, ny, nz), F32),
            pltpu.VMEM((4, 3, nl, quarter, nz), BF16),
            pltpu.VMEM((4, 3, nl, quarter, nz), BF16),
            pltpu.VMEM((3, nl, quarter, nz), BF16),
            pltpu.VMEM((3, nl, quarter, nz), BF16),
            pltpu.VMEM((3, 3, nl, quarter, nz), BF16),
            dma((4,)),
            dma((len(KINDS), 2)), dma((len(KINDS), 2)),
            dma((3, 2)), dma((3, 2)),
            dma((2,)),
            dma((4,)), dma((1,)),
            dma((2,)),
            dma((1,)), dma((3,)),
        ],
        compiler_params=pltpu.CompilerParams(
            collective_id=0, has_side_effects=True, vmem_limit_bytes=44 * 1024 * 1024),
        cost_estimate=pl.CostEstimate(flops=60_000_000, bytes_accessed=4_000_000, transcendentals=0),
    )(pltpu.with_memory_space_constraint(start_states, pltpu.HBM), pltpu.with_memory_space_constraint(base_flow, pltpu.HBM))


def solution(mesh):
    in_specs = (P("seg", None, "gx", None, None), P("seg", None, None, "gx", None, None))
    out_specs = P("seg", None, "gx", None, None)
    body = functools.partial(local, mesh.shape["seg"], mesh.shape["gx"])
    return jax.shard_map(body, mesh=mesh, in_specs=in_specs, out_specs=out_specs, check_vma=False)
```

time: 30.3 us -> 28.2 us (0.931)
  the two profiles are of different devices: /device:TPU:9 before, /device:TPU:15 now
where the time goes in v1:
time: 28.2 us; the launch traced here: 28.1 us
  Pallas kernels  27.2 us (96%)
  local copies, waits for them, and re-layouts  0.91 us (3%)
    pallas_call x1, Pallas kernels, local(): pl.pallas_call(functools.partial(kernel, n_seg, n_gx, nl, ny, nz), out_sh...  27.2 us
    unnamed x1, local copies, waits for them, and re-layouts  0.91 us

profile of v1, /device:TPU:15, one launch (start us, length us, event | category | flops | bytes accessed | tf_op | source)
XLA Modules:
  0.0 28.1 jit_solution(13494549745378296029)
XLA Ops:
  0.0 27.2 %shard_map.28 = f32[1,3,3,64,384]{4,3,2,1,0:T(8,128)S(1)} custom-call(f32[1,3,3,64,384]{4,3,2,1,0:T(8,128)} %start_ref.1, bf16[1,3,3,3,64,384]{5,4,3,2,1,0:T(8,128)(2,1)} %base_ref.1), custom_call_target="tpu_custom_call" | custom-call | flops 60000000 | bytes 4000000 | tf_op jit(solution)/shard_map/pallas_call | solution.py:461
  27.2 0.9 %copy.4 = f32[1,3,3,64,384]{4,3,2,1,0:T(8,128)} copy(f32[1,3,3,64,384]{4,3,2,1,0:T(8,128)S(1)} %shard_map.28) | data formatting | bytes 1769472

commit v2 on v1

--- a/solution.py
+++ b/solution.py
@@ -15,7 +15,8 @@
 ROWS = 16
 PAD_Q = 8
 PAD_B = 16
-RELAY_AT = 1
+ACROSS = (0, 1, 1, 2)
+FORWARD = (4, 5, 5)
 F32 = jnp.float32
 BF16 = jnp.bfloat16
 
@@ -36,7 +37,7 @@
     return jnp.where(code < 0, -size, size)
 
 
-def kernel(n_seg, n_gx, nl, ny, nz, start_ref, base_ref, out_ref, q, b, hq, hb, sq, nq, ub, gp, enc, rt, ra, rb, tq,
+def kernel(n_seg, n_gx, nl, ny, nz, start_ref, base_ref, out_ref, q, b, hq, hb, sq, nq, ub, gp, eq, enc, rt, ra, rb, tq,
            load_sem, qs_sem, qr_sem, bs_sem, br_sem, shift_sem, a_sem, ar_sem, b_sem, c_sem, cr_sem):
     seg = lax.axis_index("seg")
     gx = lax.axis_index("gx")
@@ -52,19 +53,19 @@
     def edge(s):
         return s * (nl - 1)
 
-    load_q = pltpu.make_async_copy(start_ref.at[0], q.at[0, :, :, pl.ds(PAD_Q, ny), :], load_sem.at[0])
-    load_q.start()
-    load_b = [
-        pltpu.make_async_copy(base_ref.at[0, k], b.at[k, :, :, inner_rows, :], load_sem.at[1 + k]) for k in range(3)
-    ]
-    for copy in load_b:
-        copy.start()
-
     barrier = pltpu.get_barrier_semaphore()
     for other in (left, right, across):
         pl.semaphore_signal(barrier, inc=1, device_id={"gx": other}, device_id_type=MESH)
     for d in range(1, n_seg):
         pl.semaphore_signal(barrier, inc=1, device_id={"seg": lax.rem(seg + d, n_seg)}, device_id_type=MESH)
+
+    load_edge = [pltpu.make_async_copy(start_ref.at[0, 0, edge(s)], eq.at[s], load_sem.at[4 + s]) for s in range(2)]
+    load_q = pltpu.make_async_copy(start_ref.at[0], q.at[0, :, :, pl.ds(PAD_Q, ny), :], load_sem.at[0])
+    load_b = [
+        pltpu.make_async_copy(base_ref.at[0, k], b.at[k, :, :, inner_rows, :], load_sem.at[1 + k]) for k in range(3)
+    ]
+    for copy in (*load_edge, load_q, *load_b):
+        copy.start()
 
     def neighbour(s):
         return {"gx": lax.rem(gx + n_gx - 1 + 2 * s, n_gx)}
@@ -100,6 +101,23 @@
         return pltpu.make_async_remote_copy(
             src_ref=rb, dst_ref=tq.at[j], send_sem=c_sem.at[0], recv_sem=cr_sem.at[j],
             device_id={"seg": last}, device_id_type=MESH)
+
+    wrap = (gx == 0) | (gx == n_gx - 1)
+
+    def greet(s):
+        b_copy(0, s).start()
+        q_copy("Q0", s).start()
+        b_copy(1, s).start()
+
+    for s in range(2):
+        load_edge[s].wait()
+        sq[s, 0] = eq[s].astype(BF16)
+    pl.semaphore_wait(barrier, 3 + n_seg - 1)
+    @pl.when(wrap)
+    def _():
+        greet(far)
+
+    greet(near)
 
     q[:, :, :, 0:PAD_Q, :] = jnp.zeros((2, 3, nl, PAD_Q, nz), F32)
     q[:, :, :, PAD_Q + ny:, :] = jnp.zeros((2, 3, nl, PAD_Q, nz), F32)
@@ -110,14 +128,6 @@
     wall = jnp.full((2, PAD_B, nz), 1.0, BF16)
     hb[:, 1, 0:PAD_B, :] = -wall
     hb[:, 1, PAD_B + ny:, :] = wall
-
-    load_q.wait()
-    for s in range(2):
-        sq[s, 0] = q[0, 0, edge(s), PAD_Q:PAD_Q + ny, :].astype(BF16)
-    pl.semaphore_wait(barrier, 3 + n_seg - 1)
-    for s in (far, near):
-        b_copy(0, s).start()
-        q_copy("Q0", s).start()
 
     def by_rows(chunk):
         def body(r, carry):
@@ -204,8 +214,6 @@
             sq[s, 1, pl.ds(at, ROWS), :] = totals[0].astype(BF16)
 
         by_rows(chunk)
-        q_copy("S0", s).start()
-        b_copy(1, s).start()
 
     def exchange(s):
         x, signed = edge(s), sign(s)
@@ -287,17 +295,26 @@
                 q[1, c, x, inside, :] += shares[c - 1]
 
         by_rows(add)
+
+        def chunk(at):
+            for c, total in zip((1, 2), stencil(1, x, at, (1, 2), s)):
+                q[0, c, x, pl.ds(at + PAD_Q, ROWS), :] = total + gp[s, c - 1, pl.ds(at, ROWS), :]
+
+        by_rows(chunk)
+
+    def fourth(s):
+        x, signed = edge(s), sign(s)
+        b_copy(2, 1 - s).wait_recv()
         q_copy("U", 1 - s).wait_recv()
         q_copy("H", 1 - s).wait_recv()
-        b_copy(2, 1 - s).wait_recv()
 
         def chunk(at):
             here, inside = pl.ds(at, ROWS), pl.ds(at + PAD_Q, ROWS)
             theirs = nq[s, here, :] + hq_at(s, 4, at)
             nq[s, here, :] = theirs
             weight, push = DIFFUSE - signed * hb_at(s, 2, at), signed * theirs
-            for c, total in zip((1, 2), stencil(1, x, at, (1, 2), s)):
-                total += gp[s, c - 1, here, :] + hq_at(s, 4 + c, at)
+            for c in range(1, 3):
+                total = q[0, c, x, inside, :] + hq_at(s, 4 + c, at)
                 q[0, c, x, inside, :] = total
                 sq[s, 6 + c, here, :] = (weight * total - push * b_at(2, c, x, at)).astype(BF16)
 
@@ -333,23 +350,21 @@
             flag = flag | (seg == r)
         return flag
 
-    def start_relay():
-        @pl.when(seg == 0)
-        def _():
-            z_copy(enc.at[0]).start()
-
-        @pl.when((seg != 0) & is_relay())
-        def _():
-            a_copy(0).wait_recv()
-            z_copy(ra).start()
-
-    def forward_relay():
-        @pl.when(is_relay() & (seg != last))
-        def _():
-            z_copy(ra).wait_recv()
-            for j in range(3):
+    def relay(point):
+        for j in range(4):
+            if ACROSS[j] == point:
                 @pl.when(seg == relays[j])
                 def _():
+                    if j == 0:
+                        z_copy(enc.at[0]).start()
+                    else:
+                        a_copy(j).wait_recv()
+                        z_copy(ra).start()
+        for j in range(3):
+            if FORWARD[j] == point:
+                @pl.when(seg == relays[j])
+                def _():
+                    z_copy(ra).wait_recv()
                     c_copy(j).start()
 
     def subtract_target():
@@ -380,51 +395,73 @@
                         flipped = -flipped
                     out_ref[0, c, :, j * quarter:(j + 1) * quarter, :] -= flipped.reshape(nl, quarter, nz)
 
+    load_q.wait()
     for j in range(4):
         for c in range(3):
             enc[j, c] = encode(q[0, c, :, PAD_Q + j * quarter:PAD_Q + (j + 1) * quarter, :])
 
     @pl.when(seg == 0)
     def _():
-        for j in range(1, 4):
+        for j in range(1, 3):
             a_copy(j).start()
 
-    @pl.when(seg > 0)
-    def _():
-        shift.start()
-
+    relay(0)
     load_b[0].wait()
     first(far)
+
+    @pl.when(wrap)
+    def _():
+        q_copy("S0", far).start()
+        b_copy(2, far).start()
+
     first(near)
+    q_copy("S0", near).start()
+    b_copy(2, near).start()
+
+    @pl.when(seg == 0)
+    def _():
+        a_copy(3).start()
+
+    @pl.when(seg > 0)
+    def _():
+        shift.start()
+
+    @pl.when(jnp.logical_not(wrap))
+    def _():
+        greet(far)
+        q_copy("S0", far).start()
+        b_copy(2, far).start()
+
+    relay(1)
     for x in range(1, nl - 1):
         inner(0, x)
     load_b[1].wait()
     exchange(near)
+    ahead_of(near)
+    second(near)
+    prepare(near)
     exchange(far)
-    if RELAY_AT == 0:
-        start_relay()
+    relay(2)
     ahead_of(far)
-    ahead_of(near)
-    if RELAY_AT == 1:
-        start_relay()
-    second(near)
+    relay(3)
     second(far)
-    b_copy(2, far).start()
-    b_copy(2, near).start()
-    if RELAY_AT == 2:
-        start_relay()
-    prepare(near)
+    relay(4)
     prepare(far)
     load_b[2].wait()
     third(near)
+    fourth(near)
     third(far)
+    relay(5)
+    fourth(far)
+    relay(6)
     for x in range(1, nl - 1):
         inner(1, x)
-    forward_relay()
+    relay(7)
     final(near)
     final(far)
     for x in range(1, nl - 1):
         inner(2, x)
+    relay(8)
     subtract_target()
     close(near)
     close(far)
@@ -472,12 +509,13 @@
             pltpu.VMEM((2, ny, nz), F32),
             pltpu.VMEM((2, ny, nz), F32),
             pltpu.VMEM((2, 2, ny, nz), F32),
+            pltpu.VMEM((2, ny, nz), F32),
             pltpu.VMEM((4, 3, nl, quarter, nz), BF16),
             pltpu.VMEM((4, 3, nl, quarter, nz), BF16),
             pltpu.VMEM((3, nl, quarter, nz), BF16),
             pltpu.VMEM((3, nl, quarter, nz), BF16),
             pltpu.VMEM((3, 3, nl, quarter, nz), BF16),
-            dma((4,)),
+            dma((6,)),
             dma((len(KINDS), 2)), dma((len(KINDS), 2)),
             dma((3, 2)), dma((3, 2)),
             dma((2,)),

time: 28.2 us -> 26 us (0.922)
  the two profiles are of different devices: /device:TPU:15 before, /device:TPU:9 now
where the time goes in v2:
time: 26 us; the launch traced here: 25.6 us
  Pallas kernels  24.7 us (95%)
  local copies, waits for them, and re-layouts  0.91 us (4%)
    pallas_call x1, Pallas kernels, local(): pl.pallas_call(functools.partial(kernel, n_seg, n_gx, nl, ny, nz), out_sh...  24.7 us
    unnamed x1, local copies, waits for them, and re-layouts  0.91 us

profile of v2, /device:TPU:9, one launch (start us, length us, event | category | flops | bytes accessed | tf_op | source)
XLA Modules:
  0.0 25.6 jit_solution(4524168501232487110)
XLA Ops:
  0.0 24.7 %shard_map.28 = f32[1,3,3,64,384]{4,3,2,1,0:T(8,128)S(1)} custom-call(f32[1,3,3,64,384]{4,3,2,1,0:T(8,128)} %start_ref.1, bf16[1,3,3,3,64,384]{5,4,3,2,1,0:T(8,128)(2,1)} %base_ref.1), custom_call_target="tpu_custom_call" | custom-call | flops 60000000 | bytes 4000000 | tf_op jit(solution)/shard_map/pallas_call | solution.py:498
  24.7 0.9 %copy.4 = f32[1,3,3,64,384]{4,3,2,1,0:T(8,128)} copy(f32[1,3,3,64,384]{4,3,2,1,0:T(8,128)S(1)} %shard_map.28) | data formatting | bytes 1769472

commit v3 on v2

--- a/solution.py
+++ b/solution.py
@@ -15,8 +15,8 @@
 ROWS = 16
 PAD_Q = 8
 PAD_B = 16
-ACROSS = (0, 1, 1, 2)
-FORWARD = (4, 5, 5)
+ACROSS = (0, 4, 4, 4)
+FORWARD = 4
 F32 = jnp.float32
 BF16 = jnp.bfloat16
 
@@ -38,7 +38,7 @@
 
 
 def kernel(n_seg, n_gx, nl, ny, nz, start_ref, base_ref, out_ref, q, b, hq, hb, sq, nq, ub, gp, eq, enc, rt, ra, rb, tq,
-           load_sem, qs_sem, qr_sem, bs_sem, br_sem, shift_sem, a_sem, ar_sem, b_sem, c_sem, cr_sem):
+           load_sem, qs_sem, qr_sem, bs_sem, br_sem, shift_sem, a_sem, ar_sem, z_sem, zr_sem, y_sem, c_sem):
     seg = lax.axis_index("seg")
     gx = lax.axis_index("gx")
     last = n_seg - 1
@@ -50,6 +50,12 @@
     near = 1 - far
     inner_rows = pl.ds(PAD_B, ny)
 
+    def is_relay():
+        flag = seg == 0
+        for r in relays[1:]:
+            flag = flag | (seg == r)
+        return flag
+
     def edge(s):
         return s * (nl - 1)
 
@@ -58,6 +64,14 @@
         pl.semaphore_signal(barrier, inc=1, device_id={"gx": other}, device_id_type=MESH)
     for d in range(1, n_seg):
         pl.semaphore_signal(barrier, inc=1, device_id={"seg": lax.rem(seg + d, n_seg)}, device_id_type=MESH)
+    for r in relays[1:3]:
+        @pl.when(seg == r)
+        def _():
+            pl.semaphore_signal(barrier, inc=1, device_id={"seg": last, "gx": across}, device_id_type=MESH)
+
+        @pl.when(seg == last)
+        def _():
+            pl.semaphore_signal(barrier, inc=1, device_id={"seg": r, "gx": across}, device_id_type=MESH)
 
     load_edge = [pltpu.make_async_copy(start_ref.at[0, 0, edge(s)], eq.at[s], load_sem.at[4 + s]) for s in range(2)]
     load_q = pltpu.make_async_copy(start_ref.at[0], q.at[0, :, :, pl.ds(PAD_Q, ny), :], load_sem.at[0])
@@ -92,17 +106,22 @@
             src_ref=enc.at[j], dst_ref=ra, send_sem=a_sem.at[j], recv_sem=ar_sem.at[0],
             device_id={"seg": relays[j]}, device_id_type=MESH)
 
-    def z_copy(source):
+    def z_copy(j, source):
         return pltpu.make_async_remote_copy(
-            src_ref=source, dst_ref=rb, send_sem=b_sem.at[0], recv_sem=b_sem.at[1],
+            src_ref=source, dst_ref=tq.at[j], send_sem=z_sem.at[0], recv_sem=zr_sem.at[j],
+            device_id={"seg": last, "gx": across}, device_id_type=MESH)
+
+    def y_copy():
+        return pltpu.make_async_remote_copy(
+            src_ref=enc.at[0], dst_ref=rb, send_sem=y_sem.at[0], recv_sem=y_sem.at[1],
             device_id={"gx": across}, device_id_type=MESH)
 
-    def c_copy(j):
+    def c_copy():
         return pltpu.make_async_remote_copy(
-            src_ref=rb, dst_ref=tq.at[j], send_sem=c_sem.at[0], recv_sem=cr_sem.at[j],
+            src_ref=rb, dst_ref=tq.at[0], send_sem=c_sem.at[0], recv_sem=zr_sem.at[0],
             device_id={"seg": last}, device_id_type=MESH)
 
-    wrap = (gx == 0) | (gx == n_gx - 1)
+    early = (gx == 0) | (gx == n_gx - 1) | (gx == n_gx // 2) | (gx == n_gx // 2 - 1)
 
     def greet(s):
         b_copy(0, s).start()
@@ -112,8 +131,9 @@
     for s in range(2):
         load_edge[s].wait()
         sq[s, 0] = eq[s].astype(BF16)
-    pl.semaphore_wait(barrier, 3 + n_seg - 1)
-    @pl.when(wrap)
+    met = jnp.where(seg == last, 2, jnp.where(is_relay() & (seg > 0), 1, 0))
+    pl.semaphore_wait(barrier, 3 + n_seg - 1 + met)
+    @pl.when(early)
     def _():
         greet(far)
 
@@ -344,28 +364,21 @@
 
         by_rows(chunk)
 
-    def is_relay():
-        flag = seg == 0
-        for r in relays[1:]:
-            flag = flag | (seg == r)
-        return flag
-
     def relay(point):
         for j in range(4):
             if ACROSS[j] == point:
                 @pl.when(seg == relays[j])
                 def _():
                     if j == 0:
-                        z_copy(enc.at[0]).start()
+                        y_copy().start()
                     else:
                         a_copy(j).wait_recv()
-                        z_copy(ra).start()
-        for j in range(3):
-            if FORWARD[j] == point:
-                @pl.when(seg == relays[j])
-                def _():
-                    z_copy(ra).wait_recv()
-                    c_copy(j).start()
+                        z_copy(j, ra).start()
+        if FORWARD == point:
+            @pl.when(seg == 0)
+            def _():
+                y_copy().wait_recv()
+                c_copy().start()
 
     def subtract_target():
         @pl.when(seg < last)
@@ -377,16 +390,13 @@
 
         @pl.when(seg == last)
         def _():
-            z_copy(ra).wait_recv()
-            for j in range(3):
-                c_copy(j).wait_recv()
             row = lax.broadcasted_iota(jnp.int32, (nz, nz), 0)
             column = lax.broadcasted_iota(jnp.int32, (nz, nz), 1)
             flip = jnp.where((row + column == 0) | (row + column == nz), 1.0, 0.0).astype(BF16)
             for j in range(4):
-                source = rb if j == 3 else tq.at[j]
+                z_copy(j, ra).wait_recv()
                 for c in range(3):
-                    values = decode(source[c]).reshape(nl * quarter, nz)
+                    values = decode(tq[j, c]).reshape(nl * quarter, nz)
                     high = values.astype(BF16)
                     low = (values - high.astype(F32)).astype(BF16)
                     flipped = jnp.dot(high, flip, preferred_element_type=F32)
@@ -409,7 +419,7 @@
     load_b[0].wait()
     first(far)
 
-    @pl.when(wrap)
+    @pl.when(early)
     def _():
         q_copy("S0", far).start()
         b_copy(2, far).start()
@@ -426,7 +436,7 @@
     def _():
         shift.start()
 
-    @pl.when(jnp.logical_not(wrap))
+    @pl.when(jnp.logical_not(early))
     def _():
         greet(far)
         q_copy("S0", far).start()
@@ -481,13 +491,14 @@
         for j in range(1, 4):
             a_copy(j).wait_send()
 
-    @pl.when(is_relay())
-    def _():
-        z_copy(ra).wait_send()
-
-    @pl.when(is_relay() & (seg != last))
-    def _():
-        c_copy(0).wait_send()
+    @pl.when(seg == 0)
+    def _():
+        y_copy().wait_send()
+        c_copy().wait_send()
+
+    @pl.when(is_relay() & (seg > 0))
+    def _():
+        z_copy(1, ra).wait_send()
 
 
 def local(n_seg, n_gx, start_states, base_flow):
@@ -514,14 +525,14 @@
             pltpu.VMEM((4, 3, nl, quarter, nz), BF16),
             pltpu.VMEM((3, nl, quarter, nz), BF16),
             pltpu.VMEM((3, nl, quarter, nz), BF16),
-            pltpu.VMEM((3, 3, nl, quarter, nz), BF16),
+            pltpu.VMEM((4, 3, nl, quarter, nz), BF16),
             dma((6,)),
             dma((len(KINDS), 2)), dma((len(KINDS), 2)),
             dma((3, 2)), dma((3, 2)),
             dma((2,)),
             dma((4,)), dma((1,)),
-            dma((2,)),
-            dma((1,)), dma((3,)),
+            dma((1,)), dma((4,)),
+            dma((2,)), dma((1,)),
         ],
         compiler_params=pltpu.CompilerParams(
             collective_id=0, has_side_effects=True, vmem_limit_bytes=44 * 1024 * 1024),

time: 26 us -> 25.7 us (0.988); the launches traced: 25.6 us -> 25.6 us
  no operation moved by 1% of the time
where the time goes in v3:
time: 25.7 us; the launch traced here: 25.6 us
  Pallas kernels  24.7 us (96%)
  local copies, waits for them, and re-layouts  0.91 us (4%)
    pallas_call x1, Pallas kernels, local(): pl.pallas_call(functools.partial(kernel, n_seg, n_gx, nl, ny, nz), out_sh...  24.7 us
    unnamed x1, local copies, waits for them, and re-layouts  0.91 us

profile of v3, /device:TPU:9, one launch (start us, length us, event | category | flops | bytes accessed | tf_op | source)
XLA Modules:
  0.0 25.6 jit_solution(4600784768426413624)
XLA Ops:
  0.0 24.7 %shard_map.28 = f32[1,3,3,64,384]{4,3,2,1,0:T(8,128)S(1)} custom-call(f32[1,3,3,64,384]{4,3,2,1,0:T(8,128)} %start_ref.1, bf16[1,3,3,3,64,384]{5,4,3,2,1,0:T(8,128)(2,1)} %base_ref.1), custom_call_target="tpu_custom_call" | custom-call | flops 60000000 | bytes 4000000 | tf_op jit(solution)/shard_map/pallas_call | solution.py:509
  24.7 0.9 %copy.4 = f32[1,3,3,64,384]{4,3,2,1,0:T(8,128)} copy(f32[1,3,3,64,384]{4,3,2,1,0:T(8,128)S(1)} %shard_map.28) | data formatting | bytes 1769472
